TPU v7x, 32 devices: a whole 2x2x4 slice. The times are simulated.
32 devices in a mesh: groups: 2 (over x), tensor: 16 (over z, y, core).
Axes of the slice: x: 2, y: 2, z: 4, core: 2. Of those that a mesh axis runs over, the one named last changes fastest.
Arguments:
- down_weight: bfloat16 [2, 28672, 6144], P(None, 'tensor'), may hold values from -6 to 6
- generator_left: float32 [32, 128, 128], P(('groups', 'tensor')), parts along dimension 0, may hold values from -0.5 to 0.5
- generator_right: float32 [32, 224, 224], P(('groups', 'tensor')), parts along dimension 0, may hold values from -0.375 to 0.375
- owner_map: int32 [4], P('groups'), parts along dimension 0, may hold values from 0 to 15
Outputs:
- merged: bfloat16 [4, 28672, 6144], P('groups', 'tensor'), parts along dimension 0
There are 2 independent parts, one for each index of `groups`. A program takes and returns all parts, laid end to end along the dimension named above; an argument that names none is the same for every part. Nothing has to cross between parts.
All inputs are finite; a program needn't handle non-finite values.
Results may differ from a plain program's by a relative error of at most 0.0049.
Values may be sent and summed in bfloat16 or wider, within the bound.
A program may use at most 384 MiB of HBM per device.

v0:
```python
import jax
import jax.numpy as jnp
from jax import lax
from jax.sharding import PartitionSpec as P


def broadcast(block, axis, owner):
    block = jnp.where(lax.axis_index(axis) == owner, block, jnp.zeros_like(block))
    return lax.psum(block, axis)


def cayley(raw):
    skewed = 0.5 * (raw - raw.T)
    identity = jnp.eye(raw.shape[0], dtype=raw.dtype)
    shifted = identity - skewed
    numerator = jnp.dot(shifted, shifted, precision=lax.Precision.HIGHEST)
    gramian = identity - jnp.dot(skewed, skewed, precision=lax.Precision.HIGHEST)
    lower_part = jnp.linalg.cholesky(gramian)
    return jax.scipy.linalg.cho_solve((lower_part, True), numerator)


def outer_single(factor, portion):
    extent = portion.shape
    product = jnp.dot(
        factor,
        portion.reshape(extent[0], extent[1] * extent[2]),
        precision=lax.Precision.HIGHEST,
        preferred_element_type=jnp.float32,
    )
    product = product.astype(jnp.bfloat16).reshape(extent)
    return lax.all_to_all(product, "tensor", split_axis=0, concat_axis=2, tiled=True)


def body(down_weight, generator_left, generator_right, owner_map):
    layers = down_weight.shape[0]
    columns = down_weight.shape[2]
    order_right = generator_right.shape[1]
    rows_left = down_weight.shape[1] // order_right
    own_left = cayley(generator_left[0])
    own_right = cayley(generator_right[0])
    list_left = []
    list_right = []
    for layer_index in range(layers):
        received = (
            broadcast(own_left, "tensor", owner_map[layer_index]),
            broadcast(own_right, "tensor", owner_map[layer_index]),
        )
        list_left.append(received[0])
        list_right.append(received[1])
    stacked_left = jnp.stack(list_left)
    stacked_right = jnp.stack(list_right)
    blocks = down_weight.reshape(layers, rows_left, order_right, columns)
    results = []
    for layer_index in range(layers):
        rotated = jnp.einsum(
            "bk,akc->abc",
            stacked_right[layer_index],
            blocks[layer_index],
            precision=lax.Precision.HIGHEST,
            preferred_element_type=jnp.float32,
        ).astype(jnp.bfloat16)
        merged_layer = outer_single(
            stacked_left[layer_index],
            lax.all_to_all(rotated, "tensor", split_axis=2, concat_axis=0, tiled=True),
        )
        results.append(merged_layer.reshape(rows_left * order_right, columns))
    merged = jnp.stack(results)
    return merged


def solution(mesh):
    placed = (
        P(None, "tensor", None),
        P(("groups", "tensor"), None, None),
        P(("groups", "tensor"), None, None),
        P("groups"),
    )
    return jax.shard_map(
        body, mesh=mesh, in_specs=placed, out_specs=P("groups", "tensor", None), check_vma=False
    )
```

profile of v0, /device:TPU:16, one launch (start us, length us, event | category | flops | bytes accessed | tf_op | source)
XLA Modules:
  0.0 2404.3 jit_solution(5048344083274073696)
XLA Ops:
  6.5 0.0 all-reduce.6.cloned.1.call-start
  6.5 0.9 copy.25
  7.5 1.1 fusion.32
  8.6 1.1 fusion.16
  9.8 1.1 copy.28
  10.8 1.4 fusion.2
  12.3 1.4 fusion.11
  13.7 1.3 fusion.39
  16.3 0.1 copy.27
  16.4 11.7 cholesky.57
  28.2 0.6 compare_reduce_fusion.2
  28.8 0.7 fusion.13
  29.5 9.8 custom-call.28
  39.3 0.1 copy.30
  39.4 0.1 fusion.1
  39.5 11.7 cholesky.114
  51.3 0.6 compare_reduce_fusion.1
  51.9 10.0 custom-call.29
  62.0 0.2 constant_dynamic-update-slice_fusion.1
  62.2 0.2 convolution_subtract_fusion.2
  62.4 8.8 cholesky.130
  71.2 0.7 compare_reduce_fusion
  73.2 0.1 fusion.17
  73.3 19.7 custom-call.30
  93.0 0.4 fusion.8
  93.4 0.4 convolution_subtract_fusion.1
  93.8 0.3 fusion.28
  94.0 0.2 fusion.27
  94.3 0.4 convolution_subtract_fusion
  94.7 0.4 fusion.25
  95.0 0.3 fusion.23
  95.3 0.9 broadcast_select_fusion
  96.2 0.8 fusion.7
  97.0 0.0 all-reduce.6.cloned.1.call-update
  97.0 29.5 %fusion.38 = (bf16[1,1792,6144]{2,1,0:T(8,128)(2,1)}, bf16[1,1792,6144]{2,1,0:T(8,128)(2,1)}) fusion(bf16[2,1792,6144]{2,1,0:T(8,128)(2,1)} %param.4), kind=kLoop, calls=%fused_computation.81 | loop fusion | bytes 88080384 | tf_op jit(solution)/shard_map/slice | solution.py:58
  126.5 63.0 %all-reduce.6.cloned.1.call-done = (f32[128,128]{1,0:T(8,128)}, f32[224,224]{1,0:T(8,128)}, f32[128,128]{1,0:T(8,128)}, f32[224,224]{1,0:T(8,128)}) async-done(((f32[128,128]{1,0:T(8,128)}, f32[224,224]{1,0:T(8,128)}, f32[128,128]{1,0:T(8,128)}, f32[224,224]{1,0:T(8,128)}), (f32[128,128]{1,0:T(8,128)}, f32[224,224]{1,0:T(8,128)}, f32[128,128]{1,0:T(8,128)}, ...) | async-done | bytes 532496 | tf_op jit(solution)/shard_map/psum | solution.py:9
  189.5 23.9 convert_bitcast_fusion
  213.3 33.8 %copy.35 = bf16[8,224,6144]{1,0,2:T(8,128)(2,1)} copy(bf16[8,224,6144]{2,1,0:T(8,128)(2,1)} %convert_bitcast_fusion) | data formatting | bytes 44040192 | tf_op jit(solution)/shard_map/convert_element_type | solution.py:61
  247.1 16.4 all-to-all-start.2
  263.4 0.0 copy-done
  263.5 27.8 %convert_bitcast_fusion.1 = bf16[8,224,6144]{2,1,0:T(8,128)(2,1)} fusion(bf16[8,224,6144]{2,1,0:T(8,128)(2,1)} %bitcast.131, f32[224,224]{1,0:T(8,128)S(1)} %copy-done), kind=kOutput, calls=%fused_computation.6 | convolution fusion | flops 29606019072 | bytes 44240896 | tf_op jit(solution)/shard_map/bk,akc->abc/dot_general | solution.py:55
  291.2 33.3 %copy.32 = bf16[8,224,6144]{1,0,2:T(8,128)(2,1)} copy(bf16[8,224,6144]{2,1,0:T(8,128)(2,1)} %convert_bitcast_fusion.1) | data formatting | bytes 44040192 | tf_op jit(solution)/shard_map/convert_element_type | solution.py:61
  324.5 480.9 %all-to-all-done.2 = bf16[8,224,6144]{1,0,2:T(8,128)(2,1)} async-done(((bf16[8,224,6144]{1,0,2:T(8,128)(2,1)}), bf16[8,224,6144]{1,0,2:T(8,128)(2,1)}, u32[]{:S(2)}, u32[]{:S(2)}) %all-to-all-start.2) | async-done | bytes 22020128 | tf_op jit(solution)/shard_map/all_to_all | solution.py:64
  805.4 5.4 all-to-all-start
  810.8 0.0 copy-start.2
  810.8 34.3 %copy.43 = bf16[16,8,224,384]{3,1,2,0:T(8,128)(2,1)} copy(bf16[16,8,224,384]{2,1,3,0:T(8,128)(2,1)} %bitcast.100) | data formatting | bytes 44040192
  845.2 0.0 copy-done.2
  845.2 23.6 convolution_convert_fusion
  868.8 20.4 copy.44
  889.2 463.4 %all-to-all-done = bf16[8,224,6144]{1,0,2:T(8,128)(2,1)} async-done(((bf16[8,224,6144]{1,0,2:T(8,128)(2,1)}), bf16[8,224,6144]{1,0,2:T(8,128)(2,1)}, u32[]{:S(2)}, u32[]{:S(2)}) %all-to-all-start) | async-done | bytes 22020128 | tf_op jit(solution)/shard_map/all_to_all | solution.py:64
  1352.5 5.5 all-to-all-start.3
  1358.0 0.0 copy-start.1
  1358.0 34.4 %copy.41 = bf16[16,8,224,384]{3,1,2,0:T(8,128)(2,1)} copy(bf16[16,8,224,384]{2,1,3,0:T(8,128)(2,1)} %bitcast.101) | data formatting | bytes 44040192
  1392.4 0.0 copy-done.1
  1392.4 23.5 convolution_convert_fusion.1
  1415.9 20.4 copy.42
  1436.4 395.8 %all-to-all-done.3 = bf16[128,224,384]{2,1,0:T(8,128)(2,1)} async-done(((bf16[128,224,384]{2,1,0:T(8,128)(2,1)}), bf16[128,224,384]{2,1,0:T(8,128)(2,1)}, u32[]{:S(2)}, u32[]{:S(2)}) %all-to-all-start.3) | async-done | bytes 22020128 | tf_op jit(solution)/shard_map/all_to_all | solution.py:31
  1832.1 5.3 all-to-all-start.1
  1837.4 24.2 %copy.49 = bf16[16,8,224,384]{3,0,2,1:T(8,128)(2,1)} copy(bf16[16,8,224,384]{3,2,1,0:T(8,128)(2,1)} %bitcast.30) | data formatting | bytes 44040192 | tf_op jit(solution)/shard_map/all_to_all | solution.py:31
  1861.6 31.5 %stack_reshape.7 = bf16[1,1792,6144]{2,1,0:T(8,128)(2,1)} reshape(bf16[8,224,16,384]{3,2,1,0:T(8,128)(2,1)} %bitcast.135) | data formatting | bytes 44040192 | tf_op jit(solution)/shard_map/stack;reshape | solution.py:67
  1893.1 418.8 %all-to-all-done.1 = bf16[128,224,384]{2,1,0:T(8,128)(2,1)} async-done(((bf16[128,224,384]{2,1,0:T(8,128)(2,1)}), bf16[128,224,384]{2,1,0:T(8,128)(2,1)}, u32[]{:S(2)}, u32[]{:S(2)}) %all-to-all-start.1) | async-done | bytes 22020128 | tf_op jit(solution)/shard_map/all_to_all | solution.py:31
  2311.9 24.2 %copy.50 = bf16[16,8,224,384]{3,0,2,1:T(8,128)(2,1)} copy(bf16[16,8,224,384]{3,2,1,0:T(8,128)(2,1)} %bitcast.22) | data formatting | bytes 44040192 | tf_op jit(solution)/shard_map/all_to_all | solution.py:31
  2336.1 31.4 %stack_reshape.6 = bf16[1,1792,6144]{2,1,0:T(8,128)(2,1)} reshape(bf16[8,224,16,384]{3,2,1,0:T(8,128)(2,1)} %bitcast.136) | data formatting | bytes 44040192 | tf_op jit(solution)/shard_map/stack;reshape | solution.py:67
  2367.5 29.5 %pad_maximum_fusion = bf16[2,1792,6144]{2,1,0:T(8,128)(2,1)} fusion(bf16[1,1792,6144]{2,1,0:T(8,128)(2,1)} %stack_reshape.7, bf16[1,1792,6144]{2,1,0:T(8,128)(2,1)} %stack_reshape.6), kind=kLoop, calls=%fused_computation.2 | loop fusion | flops 22020096 | bytes 88080384 | tf_op jit(solution)/shard_map/stack | solution.py:67
  (12 shorter events, 0.2 us)
Async XLA Ops:
  6.5 182.9 %all-reduce.6.cloned.1.call-start = ((), (), s32[]{:S(2)}) async-start(), calls=%async_computation.4 | async-start | bytes 1179648 | tf_op jit(solution)/shard_map/psum | solution.py:9
  247.1 16.4 copy-start
  247.1 558.3 %all-to-all-start.2 = ((bf16[8,224,6144]{1,0,2:T(8,128)(2,1)}), bf16[8,224,6144]{1,0,2:T(8,128)(2,1)}, u32[]{:S(2)}, u32[]{:S(2)}) async-start(bf16[8,224,6144]{1,0,2:T(8,128)(2,1)} %copy.35), calls=%async_computation.2 | async-start | bytes 50331648 | tf_op jit(solution)/shard_map/all_to_all | solution.py:64
  805.4 547.2 %all-to-all-start = ((bf16[8,224,6144]{1,0,2:T(8,128)(2,1)}), bf16[8,224,6144]{1,0,2:T(8,128)(2,1)}, u32[]{:S(2)}, u32[]{:S(2)}) async-start(bf16[8,224,6144]{1,0,2:T(8,128)(2,1)} %copy.32), calls=%async_computation | async-start | bytes 50331648 | tf_op jit(solution)/shard_map/all_to_all | solution.py:64
  810.8 34.3 %copy-start.2 = (f32[128,128]{1,0:T(8,128)S(1)}, f32[128,128]{1,0:T(8,128)}, u32[]{:S(2)}) copy-start(f32[128,128]{1,0:T(8,128)} %get-tuple-element.25) | copy-start | bytes 196612
  1352.5 479.6 %all-to-all-start.3 = ((bf16[128,224,384]{2,1,0:T(8,128)(2,1)}), bf16[128,224,384]{2,1,0:T(8,128)(2,1)}, u32[]{:S(2)}, u32[]{:S(2)}) async-start(bf16[128,224,384]{2,1,0:T(8,128)(2,1)} %bitcast.133), calls=%async_computation.3 | async-start | bytes 44040192 | tf_op jit(solution)/shard_map/all_to_all | solution.py:31
  1358.0 34.4 %copy-start.1 = (f32[128,128]{1,0:T(8,128)S(1)}, f32[128,128]{1,0:T(8,128)}, u32[]{:S(2)}) copy-start(f32[128,128]{1,0:T(8,128)} %get-tuple-element.27) | copy-start | bytes 196612
  1832.1 479.7 %all-to-all-start.1 = ((bf16[128,224,384]{2,1,0:T(8,128)(2,1)}), bf16[128,224,384]{2,1,0:T(8,128)(2,1)}, u32[]{:S(2)}, u32[]{:S(2)}) async-start(bf16[128,224,384]{2,1,0:T(8,128)(2,1)} %bitcast.134), calls=%async_computation.1 | async-start | bytes 44040192 | tf_op jit(solution)/shard_map/all_to_all | solution.py:31
Sparse Core Ops, SparseCore 0:
  97.1 92.2 all-reduce.5
where the time goes:
time: 2420 us; the launch traced here: 2400 us
  waiting for transfers between devices  1820 us (75%)
  local copies, waits for them, and re-layouts  321 us (13%)
  matrix products  107 us (4%)
  other arithmetic  105 us (4%)
  starting transfers between devices  32.6 us (1%)
    all_to_all x2, waiting for transfers between devices, body(): lax.all_to_all(rotated, 'tensor', split_axis=2, concat_axis=0, tiled=True)  944 us
    all_to_all x2, waiting for transfers between devices, outer_single(): lax.all_to_all(product, 'tensor', split_axis=0, concat_axis=2, tiled=True)  815 us
    unnamed x12, local copies, waits for them, and re-layouts  111 us
    convert_element_type x2, local copies, waits for them, and re-layouts, body(): rotated = jnp.einsum('bk,akc->abc', stacked_right[layer_index], blocks[la...  67 us
    psum x1, waiting for transfers between devices, broadcast(): return lax.psum(block, axis)  63 us
    another operation x2, local copies, waits for them, and re-layouts, body(): merged = jnp.stack(results)  62.9 us
    dot_general x2, matrix products, body(): jnp.einsum('bk,akc->abc', stacked_right[layer_index], blocks[layer_index]...  51.6 us
    all_to_all x2, local copies, waits for them, and re-layouts, outer_single(): lax.all_to_all(product, 'tensor', split_axis=0, concat_axis=2, tiled=True)  48.4 us
  transfers between devices with their start and end apart: 5, of which 5 were waited for; matrix products, arithmetic and copies ran while one was open for 13% of the time, Pallas kernels for 0%

commit v1 on v0

v1 whole, which is shorter than its diff:
```python
import jax
import jax.numpy as jnp
from jax import lax
from jax.experimental import pallas as pl
from jax.experimental.pallas import tpu as pltpu
from jax.sharding import PartitionSpec as P

CHUNKS = 3


def cayley(raw):
    skewed = 0.5 * (raw - raw.T)
    identity = jnp.eye(raw.shape[0], dtype=raw.dtype)
    shifted = identity - skewed
    numerator = jnp.dot(shifted, shifted, precision=lax.Precision.HIGHEST)
    gramian = identity - jnp.dot(skewed, skewed, precision=lax.Precision.HIGHEST)
    lower_part = jnp.linalg.cholesky(gramian)
    return jax.scipy.linalg.cho_solve((lower_part, True), numerator)


def copy_block(group_ref, source_ref, *refs):
    refs[-1][...] = source_ref[...].reshape(refs[-1].shape)


def pack(down_weight, group, chunk, tensor, width):
    rows = down_weight.shape[1]
    return pl.pallas_call(
        copy_block,
        grid_spec=pltpu.PrefetchScalarGridSpec(
            num_scalar_prefetch=1,
            grid=(tensor,),
            in_specs=[pl.BlockSpec((1, rows, width), lambda t, g: (g[0], 0, chunk * tensor + t))],
            out_specs=pl.BlockSpec((1, rows, width), lambda t, g: (t, 0, 0)),
        ),
        out_shape=jax.ShapeDtypeStruct((tensor, rows, width), down_weight.dtype),
        cost_estimate=pl.CostEstimate(
            flops=0, bytes_accessed=4 * tensor * rows * width, transcendentals=0
        ),
    )(group, down_weight)


def unpack(back, group, merged, chunk, shape):
    layers, tensor, rows, width = back.shape
    more = [] if merged is None else [merged]
    return pl.pallas_call(
        copy_block,
        grid_spec=pltpu.PrefetchScalarGridSpec(
            num_scalar_prefetch=1,
            grid=(layers, tensor),
            in_specs=[pl.BlockSpec((1, 1, rows, width), lambda l, t, g: (l, t, 0, 0))]
            + [pl.BlockSpec(memory_space=pl.ANY) for _ in more],
            out_specs=pl.BlockSpec((1, rows, width), lambda l, t, g: (l, 0, chunk * tensor + t)),
        ),
        out_shape=jax.ShapeDtypeStruct(shape, back.dtype),
        input_output_aliases={2: 0} if more else {},
        cost_estimate=pl.CostEstimate(
            flops=0, bytes_accessed=4 * layers * tensor * rows * width, transcendentals=0
        ),
    )(group, back, *more)


def body(groups, tensor, down_weight, generator_left, generator_right, owner_map):
    layers, rows, columns = down_weight.shape
    order_left = generator_left.shape[1]
    order_right = generator_right.shape[1]
    rows_left = rows // order_right
    own_columns = columns // tensor
    aligned = own_columns % (CHUNKS * 128) == 0
    chunks = CHUNKS if aligned else 1
    width = own_columns // chunks
    group = lax.axis_index("groups")
    me = lax.axis_index("tensor")
    which = group.reshape(1).astype(jnp.int32)

    def outgoing(chunk):
        if aligned:
            return pack(down_weight, which, chunk, tensor, width)
        weights = lax.dynamic_index_in_dim(down_weight, group, 0, keepdims=False)
        return weights.reshape(rows, tensor, width).transpose(1, 0, 2)

    def forward(send):
        block = lax.all_to_all(send, "tensor", 0, 0, tiled=True)
        return block.reshape(order_left, order_right, width)

    tie = lax.optimization_barrier
    first, raw_left, raw_right = tie((outgoing(0), generator_left[0], generator_right[0]))
    received = [forward(first)]
    own_left = cayley(raw_left)
    own_right = cayley(raw_right)
    if chunks > 1:
        send, received[0], own_left, own_right = tie(
            (outgoing(1), received[0], own_left, own_right)
        )
        received.append(forward(send))

    mine = owner_map == me
    left = jnp.where(mine[:, None, None], own_left, 0.0)
    right = jnp.where(mine[:, None, None], own_right, 0.0)
    left, right = lax.psum((left, right), "tensor")
    for chunk in range(2, chunks):
        send, received[-1], left, right = tie((outgoing(chunk), received[-1], left, right))
        received.append(forward(send))
    left = lax.all_to_all(left, "groups", 0, 0, tiled=True)
    right = lax.all_to_all(right, "groups", 0, 0, tiled=True)

    def place(back, merged, chunk):
        if aligned:
            return unpack(back, which, merged, chunk, down_weight.shape)
        return back.transpose(0, 2, 1, 3).reshape(layers, rows, columns)

    merged = None
    for chunk in range(chunks):
        block = received[chunk].astype(jnp.float32)
        outputs = []
        for target in range(groups):
            rotated = jnp.einsum(
                "bk,akc->abc", right[target], block, precision=lax.Precision.HIGHEST
            ).astype(jnp.bfloat16)
            product = jnp.einsum(
                "ak,kbc->abc", left[target], rotated.astype(jnp.float32), precision=lax.Precision.HIGHEST
            ).astype(jnp.bfloat16)
            outputs.append(product.reshape(tensor, rows, width))
        send = jnp.concatenate(outputs, axis=0)
        if chunk == 0:
            send, received[-1] = tie((send, received[-1]))
        else:
            send, back = tie((send, back))
            merged = place(back, merged, chunk - 1)
        back = lax.all_to_all(send, ("groups", "tensor"), 0, 0, tiled=True)
        back = back.reshape(groups, tensor, rows, width)
    return place(back, merged, chunks - 1)


def solution(mesh):
    groups, tensor = mesh.shape["groups"], mesh.shape["tensor"]
    placed = (
        P(None, "tensor", None),
        P(("groups", "tensor"), None, None),
        P(("groups", "tensor"), None, None),
        P("groups"),
    )

    def step(*arrays):
        return body(groups, tensor, *arrays)

    return jax.shard_map(
        step, mesh=mesh, in_specs=placed, out_specs=P("groups", "tensor", None), check_vma=False
    )
```

time: 2420 us -> 1600 us (0.66)
  waiting for transfers between devices: 1820 us -> 1110 us
  local copies, waits for them, and re-layouts: 321 us -> 48.8 us
  Pallas kernels: 0 us -> 98.4 us
  matrix products: 107 us -> 138 us
    all_to_all x4 -> x6, waiting for transfers between devices: 1760 us -> 915 us  [the longest x3 761 us: body(): back = lax.all_to_all(send, ('groups', 'tensor'), 0, 0, tiled=True)]
    psum x1, waiting for transfers between devices: 63 us -> 199 us  [body(): left, right = lax.psum((left, right), 'tensor')]
    unnamed x12 -> x4, local copies, waits for them, and re-layouts: 111 us -> 1.99 us
    pallas_call x0 -> x6, Pallas kernels: none -> 98.4 us  [the longest x3 64.1 us: unpack(): pl.pallas_call(copy_block, grid_spec=pltpu.PrefetchScalarGridSpec(num_sca...]
    another operation x2 -> x0, local copies, waits for them, and re-layouts: 62.9 us -> none  [body(): merged = jnp.stack(results)]
    all_to_all x2 -> x0, local copies, waits for them, and re-layouts: 48.4 us -> none  [outer_single(): lax.all_to_all(product, 'tensor', split_axis=0, concat_axis=2, tiled=True)]
    concatenate x0 -> x3, other arithmetic: none -> 39.3 us  [body(): send = jnp.concatenate(outputs, axis=0)]
    dot_general x4 -> x12, matrix products: 98.8 us -> 135 us  [the longest x6 78.7 us: body(): jnp.einsum('ak,kbc->abc', left[target], rotated.astype(jnp.float32), prec...]
  transfers between devices with their start and end apart: 5 -> 7, of which waited for: 5 -> 6; matrix products, arithmetic and copies ran while one was open for 13% -> 19% of each run, Pallas kernels for 0% -> 4%
where the time goes in v1:
time: 1600 us; the launch traced here: 1590 us
  waiting for transfers between devices  1110 us (69%)
  matrix products  138 us (9%)
  other arithmetic  116 us (7%)
  Pallas kernels  98.4 us (6%)
  local copies, waits for them, and re-layouts  48.8 us (3%)
  starting transfers between devices  37.4 us (2%)
  blocking collectives  17.5 us (1%)
    all_to_all x3, waiting for transfers between devices, body(): back = lax.all_to_all(send, ('groups', 'tensor'), 0, 0, tiled=True)  761 us
    psum x1, waiting for transfers between devices, body(): left, right = lax.psum((left, right), 'tensor')  199 us
    all_to_all x3, waiting for transfers between devices, forward(): block = lax.all_to_all(send, 'tensor', 0, 0, tiled=True)  154 us
    dot_general x6, matrix products, body(): jnp.einsum('ak,kbc->abc', left[target], rotated.astype(jnp.float32), prec...  78.7 us
    pallas_call x3, Pallas kernels, unpack(): pl.pallas_call(copy_block, grid_spec=pltpu.PrefetchScalarGridSpec(num_sca...  64.1 us
    dot_general x6, matrix products, body(): jnp.einsum('bk,akc->abc', right[target], block, precision=lax.Precision.H...  55.8 us
    convert_element_type x6, local copies, waits for them, and re-layouts, body(): product = jnp.einsum('ak,kbc->abc', left[target], rotated.astype(jnp.floa...  46.2 us
    another operation x10, other arithmetic, cayley(): lower_part = jnp.linalg.cholesky(gramian)  44.6 us
  transfers between devices with their start and end apart: 7, of which 6 were waited for; matrix products, arithmetic and copies ran while one was open for 19% of the time, Pallas kernels for 4%

profile of v1, /device:TPU:16, one launch (start us, length us, event | category | flops | bytes accessed | tf_op | source)
XLA Modules:
  0.0 1586.2 jit_solution(17631909342358421985)
XLA Ops:
  6.5 0.9 copy.15
  7.5 1.1 copy.16
  8.5 11.4 shard_map.48
  19.9 6.2 all-to-all-start
  26.1 11.4 shard_map.47
  38.0 11.7 cholesky.57
  49.7 0.7 compare_reduce_fusion.2
  50.4 0.6 fusion.51
  51.0 9.8 custom-call.28
  61.0 0.4 fusion.49
  61.6 11.7 cholesky.114
  73.3 10.2 custom-call.29
  84.0 8.8 cholesky.130
  92.8 0.7 compare_reduce_fusion.1
  93.5 0.7 compare_reduce_fusion
  95.7 19.7 %custom-call.30 = f32[2,128,128]{1,2,0:T(8,128)S(1)} custom-call(f32[2,128,128]{2,1,0:T(8,128)S(1)} %pad_maximum_fusion.4), custom_call_target="InvertDiagBlocksLowerTriangular" | custom-call | tf_op jit(solution)/shard_map/jit(_cho_solve)/triangular_solve | solution.py:18
  115.4 0.4 fusion.38
  115.8 0.4 fusion.46
  116.2 0.4 convolution_subtract_fusion.1
  116.5 0.3 fusion.66
  116.8 0.2 fusion.65
  117.2 0.4 convolution_subtract_fusion
  117.5 0.3 fusion.63
  118.1 0.3 fusion.60
  118.6 67.7 %all-to-all-done = bf16[16,1792,128]{2,1,0:T(8,128)(2,1)} async-done(((bf16[16,1792,128]{2,1,0:T(8,128)(2,1)}), bf16[16,1792,128]{2,1,0:T(8,128)(2,1)}, u32[]{:S(2)}, u32[]{:S(2)}) %all-to-all-start) | async-done | bytes 7340064 | tf_op jit(solution)/shard_map/all_to_all | solution.py:82
  186.2 4.8 all-to-all-start.1
  191.3 0.7 broadcast_select_fusion.1
  192.0 0.9 broadcast_select_fusion
  192.9 11.4 shard_map.46
  204.3 199.4 %all-reduce.6.cloned.1.call-done = (f32[2,128,128]{2,1,0:T(8,128)}, f32[2,224,224]{2,1,0:T(8,128)}) async-done(((f32[2,128,128]{2,1,0:T(8,128)}, f32[2,224,224]{2,1,0:T(8,128)}), (f32[2,128,128]{2,1,0:T(8,128)}, f32[2,224,224]{2,1,0:T(8,128)})) %all-reduce.6.cloned.1.call-update) | async-done | bytes 532496 | tf_op jit(solution)/shard_map/psum | solution.py:99
  403.8 7.8 all_to_all.40
  411.6 9.7 all_to_all.41
  421.3 6.3 all-to-all-start.4
  427.6 9.3 fusion.42
  436.9 13.0 fusion.33
  450.0 7.7 copy.23
  457.7 9.3 fusion.45
  467.0 13.2 fusion.30
  480.2 7.7 copy.24
  487.9 13.1 pad_maximum_fusion
  501.0 86.5 %all-to-all-done.4 = bf16[16,1792,128]{2,1,0:T(8,128)(2,1)} async-done(((bf16[16,1792,128]{2,1,0:T(8,128)(2,1)}), bf16[16,1792,128]{2,1,0:T(8,128)(2,1)}, u32[]{:S(2)}, u32[]{:S(2)}) %all-to-all-start.4) | async-done | bytes 7340064 | tf_op jit(solution)/shard_map/all_to_all | solution.py:82
  587.5 3.9 all-to-all-start.5
  591.4 9.3 fusion.40
  600.7 13.0 fusion.21
  613.8 7.7 copy.27
  621.5 9.3 fusion.43
  630.8 13.2 fusion.18
  644.0 7.7 copy.28
  651.8 13.1 pad_maximum_fusion.2
  664.9 243.2 %all-to-all-done.5 = bf16[32,1792,128]{2,1,0:T(8,128)(2,1)} async-done(((bf16[32,1792,128]{2,1,0:T(8,128)(2,1)}), bf16[32,1792,128]{2,1,0:T(8,128)(2,1)}, u32[]{:S(2)}, u32[]{:S(2)}) %all-to-all-start.5) | async-done | bytes 14680096 | tf_op jit(solution)/shard_map/all_to_all | solution.py:129
  908.1 8.2 all-to-all-start.6
  916.3 9.3 fusion.44
  925.6 13.0 fusion.24
  938.7 7.7 copy.26
  946.4 9.3 fusion.41
  955.7 13.1 fusion.27
  968.7 7.6 copy.25
  976.4 13.1 pad_maximum_fusion.1
  989.5 243.3 %all-to-all-done.6 = bf16[32,1792,128]{2,1,0:T(8,128)(2,1)} async-done(((bf16[32,1792,128]{2,1,0:T(8,128)(2,1)}), bf16[32,1792,128]{2,1,0:T(8,128)(2,1)}, u32[]{:S(2)}, u32[]{:S(2)}) %all-to-all-start.6) | async-done | bytes 14680096 | tf_op jit(solution)/shard_map/all_to_all | solution.py:129
  1232.8 8.0 all-to-all-start.7
  1240.8 21.4 %shard_map.49.refs_0_ = bf16[2,1792,6144]{2,1,0:T(8,128)(2,1)} custom-call(s32[1]{0:T(128)} %bitcast.group_ref, bf16[2,16,1792,128]{3,2,1,0:T(8,128)(2,1)} %bitcast.38.source_ref), custom_call_target="tpu_custom_call" | custom-call | bytes 29360128 | tf_op jit(solution)/shard_map/pallas_call | solution.py:45
  1262.1 21.4 %shard_map.50.refs_0_ = bf16[2,1792,6144]{2,1,0:T(8,128)(2,1)} custom-call(s32[1]{0:T(128)} %bitcast.group_ref, bf16[2,16,1792,128]{3,2,1,0:T(8,128)(2,1)} %bitcast.39.source_ref, bf16[2,1792,6144]{2,1,0:T(8,128)(2,1)} %shard_map.49.refs_0_), custom_call_target="tpu_custom_call", output_to_operand_aliasing={{}: (2, {})} | custom-call | bytes 29360128 | tf_op jit(solution)/shard_map/pallas_call | solution.py:45
  1283.5 274.0 %all-to-all-done.7 = bf16[32,1792,128]{2,1,0:T(8,128)(2,1)} async-done(((bf16[32,1792,128]{2,1,0:T(8,128)(2,1)}), bf16[32,1792,128]{2,1,0:T(8,128)(2,1)}, u32[]{:S(2)}, u32[]{:S(2)}) %all-to-all-start.7) | async-done | bytes 14680096 | tf_op jit(solution)/shard_map/all_to_all | solution.py:129
  1557.5 21.4 %shard_map.51 = bf16[2,1792,6144]{2,1,0:T(8,128)(2,1)} custom-call(s32[1]{0:T(128)} %bitcast.group_ref, bf16[2,16,1792,128]{3,2,1,0:T(8,128)(2,1)} %bitcast.40.source_ref, bf16[2,1792,6144]{2,1,0:T(8,128)(2,1)} %shard_map.50.refs_0_), custom_call_target="tpu_custom_call", output_to_operand_aliasing={{}: (2, {})} | custom-call | bytes 29360128 | tf_op jit(solution)/shard_map/pallas_call | solution.py:45
  (31 shorter events, 2.1 us)
Async XLA Ops:
  19.9 166.3 %all-to-all-start = ((bf16[16,1792,128]{2,1,0:T(8,128)(2,1)}), bf16[16,1792,128]{2,1,0:T(8,128)(2,1)}, u32[]{:S(2)}, u32[]{:S(2)}) async-start(bf16[16,1792,128]{2,1,0:T(8,128)(2,1)} %shard_map.48), calls=%async_computation | async-start | bytes 14680064 | tf_op jit(solution)/shard_map/all_to_all | solution.py:82
  186.2 4.9 copy-start
  186.2 217.5 %all-to-all-start.1 = ((bf16[16,1792,128]{2,1,0:T(8,128)(2,1)}), bf16[16,1792,128]{2,1,0:T(8,128)(2,1)}, u32[]{:S(2)}, u32[]{:S(2)}) async-start(bf16[16,1792,128]{2,1,0:T(8,128)(2,1)} %shard_map.47), calls=%async_computation.1 | async-start | bytes 14680064 | tf_op jit(solution)/shard_map/all_to_all | solution.py:82
  191.1 212.7 %all-reduce.6.cloned.1.call-start = ((), (), s32[]{:S(2)}) async-start(), calls=%async_computation.8 | async-start | bytes 1179648 | tf_op jit(solution)/shard_map/psum | solution.py:99
  421.3 166.2 %all-to-all-start.4 = ((bf16[16,1792,128]{2,1,0:T(8,128)(2,1)}), bf16[16,1792,128]{2,1,0:T(8,128)(2,1)}, u32[]{:S(2)}, u32[]{:S(2)}) async-start(bf16[16,1792,128]{2,1,0:T(8,128)(2,1)} %shard_map.46), calls=%async_computation.4 | async-start | bytes 14680064 | tf_op jit(solution)/shard_map/all_to_all | solution.py:82
  587.5 320.6 %all-to-all-start.5 = ((bf16[32,1792,128]{2,1,0:T(8,128)(2,1)}), bf16[32,1792,128]{2,1,0:T(8,128)(2,1)}, u32[]{:S(2)}, u32[]{:S(2)}) async-start(bf16[32,1792,128]{2,1,0:T(8,128)(2,1)} %pad_maximum_fusion), calls=%async_computation.5 | async-start | bytes 29360128 | tf_op jit(solution)/shard_map/all_to_all | solution.py:129
  908.1 324.7 %all-to-all-start.6 = ((bf16[32,1792,128]{2,1,0:T(8,128)(2,1)}), bf16[32,1792,128]{2,1,0:T(8,128)(2,1)}, u32[]{:S(2)}, u32[]{:S(2)}) async-start(bf16[32,1792,128]{2,1,0:T(8,128)(2,1)} %pad_maximum_fusion.2), calls=%async_computation.6 | async-start | bytes 29360128 | tf_op jit(solution)/shard_map/all_to_all | solution.py:129
  1232.8 324.7 %all-to-all-start.7 = ((bf16[32,1792,128]{2,1,0:T(8,128)(2,1)}), bf16[32,1792,128]{2,1,0:T(8,128)(2,1)}, u32[]{:S(2)}, u32[]{:S(2)}) async-start(bf16[32,1792,128]{2,1,0:T(8,128)(2,1)} %pad_maximum_fusion.1), calls=%async_computation.7 | async-start | bytes 29360128 | tf_op jit(solution)/shard_map/all_to_all | solution.py:129
Sparse Core Ops, SparseCore 0:
  195.4 208.2 all-reduce.5
